TPU v7x, 32 devices: a whole 2x2x4 slice. The times are simulated.
32 devices in a mesh: gx: 8 (over z, x), gy: 4 (over y, core).
Axes of the slice: x: 2, y: 2, z: 4, core: 2. Of those that a mesh axis runs over, the one named last changes fastest.
Arguments:
- right_side: float32 [64, 64, 256], P('gx', 'gy'), may hold values from -8 to 8
- shift: float32 [64, 64, 256], P('gx', 'gy'), may hold values from 0.05 to 0.5
- coef_x: float32 [64, 64, 256], P('gx', 'gy'), may hold values from 0.5 to 2
- coef_y: float32 [64, 64, 256], P('gx', 'gy'), may hold values from 0.5 to 2
- coef_z: float32 [64, 64, 256], P('gx', 'gy'), may hold values from 0.5 to 2
- low_frac: float32 [2], replicated, may hold values from 0.01 to 0.05
- high_frac: float32 [2], replicated, may hold values from 1 to 1.3
Outputs:
- pressure: float32 [64, 64, 256], P('gx', 'gy')
- residual: float32 [64, 64, 256], P('gx', 'gy')
All inputs are finite; a program needn't handle non-finite values.
Results may differ from a plain program's by a relative error of at most 0.000065.
Values sent between devices are 32-bit elements; how exact they have to be, the bound alone decides.
A program may use at most 64 MiB of HBM per device.

v0:
```python
import jax
import jax.numpy as jnp
from jax import lax
from jax.sharding import PartitionSpec as P

ITERS = 8


def padded_2(cells, sides, width):
    for axis, dim in sides:
        count = lax.axis_size(axis)
        ends = count - 1
        head = lax.slice_in_dim(cells, 0, width, axis=dim)
        tail = lax.slice_in_dim(cells, cells.shape[dim] - width, cells.shape[dim], axis=dim)
        cells = jnp.concatenate(
            [
                lax.ppermute(tail, axis, [(i, (i + 1) % count) for i in range(ends)]),
                cells,
                lax.ppermute(head, axis, [((i + 1) % count, i) for i in range(ends)]),
            ],
            axis=dim,
        )
    return cells


def passed_along(array, axis, by):
    length = lax.axis_size(axis)
    pairs = [(i, i + by) for i in range(length) if 0 <= i + by < length]
    return lax.ppermute(array, axis, pairs)


def from_partner(array, axis, apart):
    return lax.ppermute(array, axis, [(i, i ^ 1 << apart) for i in range(lax.axis_size(axis))])


def lower_local(a, axis):
    width = [(0, 0)] * a.ndim
    width[axis] = (1, 0)
    return jnp.pad(a, width)[
        tuple((slice(0, -1) if k == axis else slice(None) for k in range(a.ndim)))
    ]


def upper_local(a, axis):
    width = [(0, 0)] * a.ndim
    width[axis] = (0, 1)
    return jnp.pad(a, width)[
        tuple((slice(1, None) if k == axis else slice(None) for k in range(a.ndim)))
    ]


def operate(field, shift, coef_x, coef_y, coef_z, low_x, low_y, low_z):
    padded = padded_2(field, (("gx", 1), ("gy", 2)), 1)
    total = shift * field
    total = total + coef_x * (field - padded[:, 2:, 1:-1]) + low_x * (field - padded[:, :-2, 1:-1])
    total = total + coef_y * (field - padded[:, 1:-1, 2:]) + low_y * (field - padded[:, 1:-1, :-2])
    total = (
        total + coef_z * (field - upper_local(field, 3)) + low_z * (field - lower_local(field, 3))
    )
    return total


def shards(right_side, shift, coef_x, coef_y, coef_z, low_frac, high_frac):
    before_x = passed_along(coef_x[-1:], "gx", 1)
    before_y = passed_along(coef_y[:, -1:], "gy", 1)
    low_x = jnp.concatenate([before_x, coef_x[:-1]], 0)
    low_y = jnp.concatenate([before_y, coef_y[:, :-1]], 1)
    low_z = lower_local(coef_z, 2)
    bound = lax.pmax(
        jnp.max(shift + 2.0 * (coef_x + low_x + coef_y + low_y + coef_z + low_z)), ("gx", "gy")
    )
    partner = right_side
    for bit in range(lax.axis_size("gx").bit_length() - 1):
        partner = from_partner(partner, "gx", bit)
    mirrored = jnp.flip(partner, 0)
    fields = jnp.stack([(right_side + mirrored) / 2.0, (right_side - mirrored) / 2.0])
    lmin = (low_frac * bound)[:, None, None, None]
    lmax = (high_frac * bound)[:, None, None, None]
    theta = (lmax + lmin) / 2.0
    delta = (lmax - lmin) / 2.0
    sigma = theta / delta
    rho = 1.0 / sigma
    solution = jnp.zeros_like(fields)
    resid = fields
    direction = resid / theta
    for step in range(ITERS):
        solution = solution + direction
        resid = resid - operate(direction, shift, coef_x, coef_y, coef_z, low_x, low_y, low_z)
        rho_new = 1.0 / (2.0 * sigma - rho)
        direction = rho_new * rho * direction + 2.0 * rho_new / delta * resid
        rho = rho_new
    return (solution[0] + solution[1], resid[0] + resid[1])


def solution(mesh):
    placed = (
        P("gx", "gy", None),
        P("gx", "gy", None),
        P("gx", "gy", None),
        P("gx", "gy", None),
        P("gx", "gy", None),
        P(),
        P(),
    )
    return jax.shard_map(
        shards,
        mesh=mesh,
        in_specs=placed,
        out_specs=(P("gx", "gy", None), P("gx", "gy", None)),
        check_vma=False,
    )
```

profile of v0, /device:TPU:1, one launch (start us, length us, event | category | flops | bytes accessed | tf_op | source)
XLA Modules:
  0.0 197.9 jit_solution(7488949561192880569)
XLA Ops:
  0.6 2.1 %collective-permute-start = (f32[8,16,256]{2,1,0:T(8,128)}, f32[8,16,256]{2,1,0:T(8,128)S(1)}, u32[]{:S(2)}, u32[]{:S(2)}) collective-permute-start(f32[8,16,256]{2,1,0:T(8,128)} %param.7), channel_id=1, source_target_pairs={{0,4},{4,0},{8,12},{12,8},{16,20},{20,16},{24,28},{28,24},{1,5},{5... | collective-permute-start | bytes 393224 | tf_op jit(solution)/shard_map/ppermute | solution.py:33
  3.5 2.0 %collective-permute-start.3 = (f32[1,16,256]{2,1,0:T(8,128)S(1)}, f32[1,16,256]{2,1,0:T(8,128)S(1)}, u32[]{:S(2)}, u32[]{:S(2)}) collective-permute-start(f32[1,16,256]{2,1,0:T(8,128)S(1)} %slice.299), channel_id=1, source_target_pairs={{0,4},{4,8},{8,12},{12,16},{16,20},{20,24},{24,28},{1,5},{5,9},{9,... | collective-permute-start | bytes 49160 | tf_op jit(solution)/shard_map/ppermute | solution.py:29
  6.4 4.6 %collective-permute-start.4 = (f32[8,1,256]{2,1,0:T(1,128)S(1)}, f32[8,1,256]{2,1,0:T(1,128)S(1)}, u32[]{:S(2)}, u32[]{:S(2)}) collective-permute-start(f32[8,1,256]{2,1,0:T(1,128)S(1)} %slice.301), channel_id=1, source_target_pairs={{0,1},{1,2},{2,3},{4,5},{5,6},{6,7},{8,9},{9,10},{10,11},{12,13},{... | collective-permute-start | bytes 24584 | tf_op jit(solution)/shard_map/ppermute | solution.py:29
  11.0 1.4 collective-permute-start.1
  12.4 1.9 add_reduce_fusion
  14.4 40.9 %pmax.7 = f32[]{:T(128)} all-reduce(f32[]{:T(128)} %get-tuple-element.29), channel_id=1, replica_groups=mesh['gx'=8,'gy'=4] {'gx','gy'}, use_global_device_ids=true, to_apply=%region_1.2 | all-reduce | flops 1 | bytes 8 | tf_op jit(solution)/shard_map/pmax | solution.py:69
  56.4 7.3 %collective-permute-done.2 = f32[8,16,256]{2,1,0:T(8,128)S(1)} collective-permute-done((f32[8,16,256]{2,1,0:T(8,128)S(1)}, f32[8,16,256]{2,1,0:T(8,128)S(1)}, u32[]{:S(2)}, u32[]{:S(2)}) %collective-permute-start.2) | collective-permute-done | bytes 131104 | tf_op jit(solution)/shard_map/ppermute | solution.py:33
  63.9 1.3 collective-permute-start.6
  65.2 1.3 collective-permute-start.5
  66.6 3.3 %collective-permute-done.5 = f32[2,1,16,256]{3,2,1,0:T(8,128)S(1)} collective-permute-done((f32[2,1,16,256]{3,2,1,0:T(8,128)S(1)}, f32[2,1,16,256]{3,2,1,0:T(8,128)S(1)}, u32[]{:S(2)}, u32[]{:S(2)}) %collective-permute-start.5) | collective-permute-done | bytes 32800 | tf_op jit(solution)/shard_map/ppermute | solution.py:19
  69.9 5.7 %collective-permute-start.7 = (f32[2,10,1,256]{3,2,1,0:T(1,128)S(1)}, f32[2,10,1,256]{3,2,1,0:T(1,128)S(1)}, u32[]{:S(2)}, u32[]{:S(2)}) collective-permute-start(f32[2,10,1,256]{3,2,1,0:T(1,128)S(1)} %get-tuple-element.45), channel_id=1, source_target_pairs={{1,0},{2,1},{3,2},{5,4},{6,5},{7,6},{9,8},{10,9},{11,10},{13,12},{... | collective-permute-start | bytes 61448 | tf_op jit(solution)/shard_map/ppermute | solution.py:19
  75.6 3.1 %collective-permute-start.8 = (f32[2,10,1,256]{3,2,1,0:T(1,128)S(1)}, f32[2,10,1,256]{3,2,1,0:T(1,128)S(1)}, u32[]{:S(2)}, u32[]{:S(2)}) collective-permute-start(f32[2,10,1,256]{3,2,1,0:T(1,128)S(1)} %get-tuple-element.46), channel_id=1, source_target_pairs={{0,1},{1,2},{2,3},{4,5},{5,6},{6,7},{8,9},{9,10},{10,11},{12,13},{... | collective-permute-start | bytes 61448 | tf_op jit(solution)/shard_map/ppermute | solution.py:17
  80.0 2.5 %collective-permute-start.10 = (f32[2,1,16,256]{3,2,1,0:T(8,128)S(1)}, f32[2,1,16,256]{3,2,1,0:T(8,128)S(1)}, u32[]{:S(2)}, u32[]{:S(2)}) collective-permute-start(f32[2,1,16,256]{3,2,1,0:T(8,128)S(1)} %get-tuple-element.59), channel_id=1, source_target_pairs={{0,4},{4,8},{8,12},{12,16},{16,20},{20,24},{24,28},{1,5},{5,9},{9,... | collective-permute-start | bytes 98312 | tf_op jit(solution)/shard_map/ppermute | solution.py:17
  82.6 1.3 collective-permute-start.9
  83.9 3.9 %collective-permute-done.9 = f32[2,1,16,256]{3,2,1,0:T(8,128)S(1)} collective-permute-done((f32[2,1,16,256]{3,2,1,0:T(8,128)S(1)}, f32[2,1,16,256]{3,2,1,0:T(8,128)S(1)}, u32[]{:S(2)}, u32[]{:S(2)}) %collective-permute-start.9) | collective-permute-done | bytes 32800 | tf_op jit(solution)/shard_map/ppermute | solution.py:19
  87.8 2.3 %collective-permute-start.11 = (f32[2,10,1,256]{3,2,1,0:T(1,128)S(1)}, f32[2,10,1,256]{3,2,1,0:T(1,128)S(1)}, u32[]{:S(2)}, u32[]{:S(2)}) collective-permute-start(f32[2,10,1,256]{3,2,1,0:T(1,128)S(1)} %get-tuple-element.43), channel_id=1, source_target_pairs={{1,0},{2,1},{3,2},{5,4},{6,5},{7,6},{9,8},{10,9},{11,10},{13,12},{... | collective-permute-start | bytes 61448 | tf_op jit(solution)/shard_map/ppermute | solution.py:19
  90.1 4.7 %collective-permute-start.12 = (f32[2,10,1,256]{3,2,1,0:T(1,128)S(1)}, f32[2,10,1,256]{3,2,1,0:T(1,128)S(1)}, u32[]{:S(2)}, u32[]{:S(2)}) collective-permute-start(f32[2,10,1,256]{3,2,1,0:T(1,128)S(1)} %get-tuple-element.44), channel_id=1, source_target_pairs={{0,1},{1,2},{2,3},{4,5},{5,6},{6,7},{8,9},{9,10},{10,11},{12,13},{... | collective-permute-start | bytes 61448 | tf_op jit(solution)/shard_map/ppermute | solution.py:17
  94.9 0.9 collective-permute-done.12
  96.1 2.5 %collective-permute-start.14 = (f32[2,1,16,256]{3,2,1,0:T(8,128)S(1)}, f32[2,1,16,256]{3,2,1,0:T(8,128)S(1)}, u32[]{:S(2)}, u32[]{:S(2)}) collective-permute-start(f32[2,1,16,256]{3,2,1,0:T(8,128)S(1)} %get-tuple-element.57), channel_id=1, source_target_pairs={{0,4},{4,8},{8,12},{12,16},{16,20},{20,24},{24,28},{1,5},{5,9},{9,... | collective-permute-start | bytes 98312 | tf_op jit(solution)/shard_map/ppermute | solution.py:17
  98.6 1.3 collective-permute-start.13
  99.9 3.3 %collective-permute-done.13 = f32[2,1,16,256]{3,2,1,0:T(8,128)S(1)} collective-permute-done((f32[2,1,16,256]{3,2,1,0:T(8,128)S(1)}, f32[2,1,16,256]{3,2,1,0:T(8,128)S(1)}, u32[]{:S(2)}, u32[]{:S(2)}) %collective-permute-start.13) | collective-permute-done | bytes 32800 | tf_op jit(solution)/shard_map/ppermute | solution.py:19
  103.3 1.9 collective-permute-start.15
  105.2 5.6 %collective-permute-start.16 = (f32[2,10,1,256]{3,2,1,0:T(1,128)S(1)}, f32[2,10,1,256]{3,2,1,0:T(1,128)S(1)}, u32[]{:S(2)}, u32[]{:S(2)}) collective-permute-start(f32[2,10,1,256]{3,2,1,0:T(1,128)S(1)} %get-tuple-element.42), channel_id=1, source_target_pairs={{0,1},{1,2},{2,3},{4,5},{5,6},{6,7},{8,9},{9,10},{10,11},{12,13},{... | collective-permute-start | bytes 61448 | tf_op jit(solution)/shard_map/ppermute | solution.py:17
  112.1 3.4 %collective-permute-start.18 = (f32[2,1,16,256]{3,2,1,0:T(8,128)S(1)}, f32[2,1,16,256]{3,2,1,0:T(8,128)S(1)}, u32[]{:S(2)}, u32[]{:S(2)}) collective-permute-start(f32[2,1,16,256]{3,2,1,0:T(8,128)S(1)} %get-tuple-element.55), channel_id=1, source_target_pairs={{0,4},{4,8},{8,12},{12,16},{16,20},{20,24},{24,28},{1,5},{5,9},{9,... | collective-permute-start | bytes 98312 | tf_op jit(solution)/shard_map/ppermute | solution.py:17
  115.6 1.3 collective-permute-start.17
  116.9 3.3 %collective-permute-done.17 = f32[2,1,16,256]{3,2,1,0:T(8,128)S(1)} collective-permute-done((f32[2,1,16,256]{3,2,1,0:T(8,128)S(1)}, f32[2,1,16,256]{3,2,1,0:T(8,128)S(1)}, u32[]{:S(2)}, u32[]{:S(2)}) %collective-permute-start.17) | collective-permute-done | bytes 32800 | tf_op jit(solution)/shard_map/ppermute | solution.py:19
  120.3 1.9 collective-permute-start.19
  122.2 5.6 %collective-permute-start.20 = (f32[2,10,1,256]{3,2,1,0:T(1,128)S(1)}, f32[2,10,1,256]{3,2,1,0:T(1,128)S(1)}, u32[]{:S(2)}, u32[]{:S(2)}) collective-permute-start(f32[2,10,1,256]{3,2,1,0:T(1,128)S(1)} %get-tuple-element.40), channel_id=1, source_target_pairs={{0,1},{1,2},{2,3},{4,5},{5,6},{6,7},{8,9},{9,10},{10,11},{12,13},{... | collective-permute-start | bytes 61448 | tf_op jit(solution)/shard_map/ppermute | solution.py:17
  129.1 3.9 %collective-permute-start.22 = (f32[2,1,16,256]{3,2,1,0:T(8,128)S(1)}, f32[2,1,16,256]{3,2,1,0:T(8,128)S(1)}, u32[]{:S(2)}, u32[]{:S(2)}) collective-permute-start(f32[2,1,16,256]{3,2,1,0:T(8,128)S(1)} %get-tuple-element.53), channel_id=1, source_target_pairs={{0,4},{4,8},{8,12},{12,16},{16,20},{20,24},{24,28},{1,5},{5,9},{9,... | collective-permute-start | bytes 98312 | tf_op jit(solution)/shard_map/ppermute | solution.py:17
  133.0 1.3 collective-permute-start.21
  134.3 3.6 %collective-permute-done.21 = f32[2,1,16,256]{3,2,1,0:T(8,128)S(1)} collective-permute-done((f32[2,1,16,256]{3,2,1,0:T(8,128)S(1)}, f32[2,1,16,256]{3,2,1,0:T(8,128)S(1)}, u32[]{:S(2)}, u32[]{:S(2)}) %collective-permute-start.21) | collective-permute-done | bytes 32800 | tf_op jit(solution)/shard_map/ppermute | solution.py:19
  138.0 1.9 collective-permute-start.23
  139.9 5.4 %collective-permute-start.24 = (f32[2,10,1,256]{3,2,1,0:T(1,128)S(1)}, f32[2,10,1,256]{3,2,1,0:T(1,128)S(1)}, u32[]{:S(2)}, u32[]{:S(2)}) collective-permute-start(f32[2,10,1,256]{3,2,1,0:T(1,128)S(1)} %get-tuple-element.38), channel_id=1, source_target_pairs={{0,1},{1,2},{2,3},{4,5},{5,6},{6,7},{8,9},{9,10},{10,11},{12,13},{... | collective-permute-start | bytes 61448 | tf_op jit(solution)/shard_map/ppermute | solution.py:17
  146.5 4.5 %collective-permute-start.26 = (f32[2,1,16,256]{3,2,1,0:T(8,128)S(1)}, f32[2,1,16,256]{3,2,1,0:T(8,128)S(1)}, u32[]{:S(2)}, u32[]{:S(2)}) collective-permute-start(f32[2,1,16,256]{3,2,1,0:T(8,128)S(1)} %get-tuple-element.51), channel_id=1, source_target_pairs={{0,4},{4,8},{8,12},{12,16},{16,20},{20,24},{24,28},{1,5},{5,9},{9,... | collective-permute-start | bytes 98312 | tf_op jit(solution)/shard_map/ppermute | solution.py:17
  151.1 1.3 collective-permute-start.25
  152.4 3.3 %collective-permute-done.25 = f32[2,1,16,256]{3,2,1,0:T(8,128)S(1)} collective-permute-done((f32[2,1,16,256]{3,2,1,0:T(8,128)S(1)}, f32[2,1,16,256]{3,2,1,0:T(8,128)S(1)}, u32[]{:S(2)}, u32[]{:S(2)}) %collective-permute-start.25) | collective-permute-done | bytes 32800 | tf_op jit(solution)/shard_map/ppermute | solution.py:19
  155.8 1.9 collective-permute-start.27
  157.7 5.6 %collective-permute-start.28 = (f32[2,10,1,256]{3,2,1,0:T(1,128)S(1)}, f32[2,10,1,256]{3,2,1,0:T(1,128)S(1)}, u32[]{:S(2)}, u32[]{:S(2)}) collective-permute-start(f32[2,10,1,256]{3,2,1,0:T(1,128)S(1)} %get-tuple-element.36), channel_id=1, source_target_pairs={{0,1},{1,2},{2,3},{4,5},{5,6},{6,7},{8,9},{9,10},{10,11},{12,13},{... | collective-permute-start | bytes 61448 | tf_op jit(solution)/shard_map/ppermute | solution.py:17
  164.6 3.0 %collective-permute-start.30 = (f32[2,1,16,256]{3,2,1,0:T(8,128)S(1)}, f32[2,1,16,256]{3,2,1,0:T(8,128)S(1)}, u32[]{:S(2)}, u32[]{:S(2)}) collective-permute-start(f32[2,1,16,256]{3,2,1,0:T(8,128)S(1)} %get-tuple-element.49), channel_id=1, source_target_pairs={{0,4},{4,8},{8,12},{12,16},{16,20},{20,24},{24,28},{1,5},{5,9},{9,... | collective-permute-start | bytes 98312 | tf_op jit(solution)/shard_map/ppermute | solution.py:17
  167.6 1.3 collective-permute-start.29
  168.9 3.3 %collective-permute-done.29 = f32[2,1,16,256]{3,2,1,0:T(8,128)S(1)} collective-permute-done((f32[2,1,16,256]{3,2,1,0:T(8,128)S(1)}, f32[2,1,16,256]{3,2,1,0:T(8,128)S(1)}, u32[]{:S(2)}, u32[]{:S(2)}) %collective-permute-start.29) | collective-permute-done | bytes 32800 | tf_op jit(solution)/shard_map/ppermute | solution.py:19
  172.2 1.9 collective-permute-start.31
  174.2 5.6 %collective-permute-start.32 = (f32[2,10,1,256]{3,2,1,0:T(1,128)S(1)}, f32[2,10,1,256]{3,2,1,0:T(1,128)S(1)}, u32[]{:S(2)}, u32[]{:S(2)}) collective-permute-start(f32[2,10,1,256]{3,2,1,0:T(1,128)S(1)} %get-tuple-element.34), channel_id=1, source_target_pairs={{0,1},{1,2},{2,3},{4,5},{5,6},{6,7},{8,9},{9,10},{10,11},{12,13},{... | collective-permute-start | bytes 61448 | tf_op jit(solution)/shard_map/ppermute | solution.py:17
  181.2 2.5 %collective-permute-start.34 = (f32[2,1,16,256]{3,2,1,0:T(8,128)S(1)}, f32[2,1,16,256]{3,2,1,0:T(8,128)S(1)}, u32[]{:S(2)}, u32[]{:S(2)}) collective-permute-start(f32[2,1,16,256]{3,2,1,0:T(8,128)S(1)} %get-tuple-element.47), channel_id=1, source_target_pairs={{0,4},{4,8},{8,12},{12,16},{16,20},{20,24},{24,28},{1,5},{5,9},{9,... | collective-permute-start | bytes 98312 | tf_op jit(solution)/shard_map/ppermute | solution.py:17
  183.8 1.3 collective-permute-start.33
  185.1 3.3 %collective-permute-done.33 = f32[2,1,16,256]{3,2,1,0:T(8,128)S(1)} collective-permute-done((f32[2,1,16,256]{3,2,1,0:T(8,128)S(1)}, f32[2,1,16,256]{3,2,1,0:T(8,128)S(1)}, u32[]{:S(2)}, u32[]{:S(2)}) %collective-permute-start.33) | collective-permute-done | bytes 32800 | tf_op jit(solution)/shard_map/ppermute | solution.py:19
  188.5 1.9 collective-permute-start.35
  190.4 5.6 %collective-permute-start.36 = (f32[2,10,1,256]{3,2,1,0:T(1,128)S(1)}, f32[2,10,1,256]{3,2,1,0:T(1,128)S(1)}, u32[]{:S(2)}, u32[]{:S(2)}) collective-permute-start(f32[2,10,1,256]{3,2,1,0:T(1,128)S(1)} %get-tuple-element.32), channel_id=1, source_target_pairs={{0,1},{1,2},{2,3},{4,5},{5,6},{6,7},{8,9},{9,10},{10,11},{12,13},{... | collective-permute-start | bytes 61448 | tf_op jit(solution)/shard_map/ppermute | solution.py:17
  (77 shorter events, 12.8 us)
Async XLA Ops:
  0.6 10.4 %collective-permute-start = (f32[8,16,256]{2,1,0:T(8,128)}, f32[8,16,256]{2,1,0:T(8,128)S(1)}, u32[]{:S(2)}, u32[]{:S(2)}) collective-permute-start(f32[8,16,256]{2,1,0:T(8,128)} %param.7), channel_id=1, source_target_pairs={{0,4},{4,0},{8,12},{12,8},{16,20},{20,16},{24,28},{28,24},{1,5},{5... | collective-permute-start | bytes 393224 | tf_op jit(solution)/shard_map/ppermute | solution.py:33
  3.5 8.9 %copy-start = (f32[8,16,256]{2,1,0:T(8,128)S(1)}, f32[8,16,256]{2,1,0:T(8,128)}, u32[]{:S(2)}) copy-start(f32[8,16,256]{2,1,0:T(8,128)} %param.10) | copy-start | bytes 393220
  3.5 8.9 %collective-permute-start.3 = (f32[1,16,256]{2,1,0:T(8,128)S(1)}, f32[1,16,256]{2,1,0:T(8,128)S(1)}, u32[]{:S(2)}, u32[]{:S(2)}) collective-permute-start(f32[1,16,256]{2,1,0:T(8,128)S(1)} %slice.299), channel_id=1, source_target_pairs={{0,4},{4,8},{8,12},{12,16},{16,20},{20,24},{24,28},{1,5},{5,9},{9,... | collective-permute-start | bytes 49160 | tf_op jit(solution)/shard_map/ppermute | solution.py:29
  6.4 6.0 %slice-start = ((f32[8,16,256]{2,1,0:T(8,128)}), f32[7,16,256]{2,1,0:T(8,128)S(1)}, s32[]{:S(2)}) async-start(f32[8,16,256]{2,1,0:T(8,128)} %param.9), calls=%async_computation | async-start | bytes 229376 | tf_op jit(solution)/shard_map/slice | solution.py:66
  6.4 6.0 %collective-permute-start.4 = (f32[8,1,256]{2,1,0:T(1,128)S(1)}, f32[8,1,256]{2,1,0:T(1,128)S(1)}, u32[]{:S(2)}, u32[]{:S(2)}) collective-permute-start(f32[8,1,256]{2,1,0:T(1,128)S(1)} %slice.301), channel_id=1, source_target_pairs={{0,1},{1,2},{2,3},{4,5},{5,6},{6,7},{8,9},{9,10},{10,11},{12,13},{... | collective-permute-start | bytes 24584 | tf_op jit(solution)/shard_map/ppermute | solution.py:29
  11.0 44.3 %collective-permute-start.1 = (f32[8,16,256]{2,1,0:T(8,128)S(1)}, f32[8,16,256]{2,1,0:T(8,128)S(1)}, u32[]{:S(2)}, u32[]{:S(2)}) collective-permute-start(f32[8,16,256]{2,1,0:T(8,128)S(1)} %collective-permute-done), channel_id=1, source_target_pairs={{0,8},{4,12},{8,0},{12,4},{16,24},{20,28},{24,16},{28,20},{1,9},{5... | collective-permute-start | bytes 393224 | tf_op jit(solution)/shard_map/ppermute | solution.py:33
  12.4 51.4 %copy-start.4 = (f32[8,16,256]{2,1,0:T(8,128)S(1)}, f32[8,16,256]{2,1,0:T(8,128)}, u32[]{:S(2)}) copy-start(f32[8,16,256]{2,1,0:T(8,128)} %param.7) | copy-start | bytes 393220
  14.3 41.4 %copy-start.5 = (f32[2]{0:T(128)S(1)}, f32[2]{0:T(128)}, u32[]{:S(2)}) copy-start(f32[2]{0:T(128)} %param.12) | copy-start | bytes 28
  14.4 41.4 %copy-start.6 = (f32[2]{0:T(128)S(1)}, f32[2]{0:T(128)}, u32[]{:S(2)}) copy-start(f32[2]{0:T(128)} %param.13) | copy-start | bytes 28
  55.3 8.5 %collective-permute-start.2 = (f32[8,16,256]{2,1,0:T(8,128)S(1)}, f32[8,16,256]{2,1,0:T(8,128)S(1)}, u32[]{:S(2)}, u32[]{:S(2)}) collective-permute-start(f32[8,16,256]{2,1,0:T(8,128)S(1)} %collective-permute-done.1), channel_id=1, source_target_pairs={{0,16},{4,20},{8,24},{12,28},{16,0},{20,4},{24,8},{28,12},{1,17},{... | collective-permute-start | bytes 393224 | tf_op jit(solution)/shard_map/ppermute | solution.py:33
  63.9 2.7 %collective-permute-start.6 = (f32[2,1,16,256]{3,2,1,0:T(8,128)S(1)}, f32[2,1,16,256]{3,2,1,0:T(8,128)S(1)}, u32[]{:S(2)}, u32[]{:S(2)}) collective-permute-start(f32[2,1,16,256]{3,2,1,0:T(8,128)S(1)} %get-tuple-element.61), channel_id=1, source_target_pairs={{0,4},{4,8},{8,12},{12,16},{16,20},{20,24},{24,28},{1,5},{5,9},{9,... | collective-permute-start | bytes 98312 | tf_op jit(solution)/shard_map/ppermute | solution.py:17
  65.2 4.7 %collective-permute-start.5 = (f32[2,1,16,256]{3,2,1,0:T(8,128)S(1)}, f32[2,1,16,256]{3,2,1,0:T(8,128)S(1)}, u32[]{:S(2)}, u32[]{:S(2)}) collective-permute-start(f32[2,1,16,256]{3,2,1,0:T(8,128)S(1)} %get-tuple-element.62), channel_id=1, source_target_pairs={{4,0},{8,4},{12,8},{16,12},{20,16},{24,20},{28,24},{5,1},{9,5},{13... | collective-permute-start | bytes 98312 | tf_op jit(solution)/shard_map/ppermute | solution.py:19
  66.5 13.1 %copy-start.1 = (f32[8,16,256]{2,1,0:T(8,128)S(1)}, f32[8,16,256]{2,1,0:T(8,128)}, u32[]{:S(2)}) copy-start(f32[8,16,256]{2,1,0:T(8,128)} %param.9) | copy-start | bytes 393220
  66.5 13.1 %copy-start.2 = (f32[8,16,256]{2,1,0:T(8,128)S(1)}, f32[8,16,256]{2,1,0:T(8,128)}, u32[]{:S(2)}) copy-start(f32[8,16,256]{2,1,0:T(8,128)} %param.8) | copy-start | bytes 393220
  66.6 13.1 %copy-start.3 = (f32[8,16,256]{2,1,0:T(8,128)S(1)}, f32[8,16,256]{2,1,0:T(8,128)}, u32[]{:S(2)}) copy-start(f32[8,16,256]{2,1,0:T(8,128)} %param.11) | copy-start | bytes 393220
  69.9 8.9 %collective-permute-start.7 = (f32[2,10,1,256]{3,2,1,0:T(1,128)S(1)}, f32[2,10,1,256]{3,2,1,0:T(1,128)S(1)}, u32[]{:S(2)}, u32[]{:S(2)}) collective-permute-start(f32[2,10,1,256]{3,2,1,0:T(1,128)S(1)} %get-tuple-element.45), channel_id=1, source_target_pairs={{1,0},{2,1},{3,2},{5,4},{6,5},{7,6},{9,8},{10,9},{11,10},{13,12},{... | collective-permute-start | bytes 61448 | tf_op jit(solution)/shard_map/ppermute | solution.py:19
  75.6 4.0 %collective-permute-start.8 = (f32[2,10,1,256]{3,2,1,0:T(1,128)S(1)}, f32[2,10,1,256]{3,2,1,0:T(1,128)S(1)}, u32[]{:S(2)}, u32[]{:S(2)}) collective-permute-start(f32[2,10,1,256]{3,2,1,0:T(1,128)S(1)} %get-tuple-element.46), channel_id=1, source_target_pairs={{0,1},{1,2},{2,3},{4,5},{5,6},{6,7},{8,9},{9,10},{10,11},{12,13},{... | collective-permute-start | bytes 61448 | tf_op jit(solution)/shard_map/ppermute | solution.py:17
  80.0 3.9 %collective-permute-start.10 = (f32[2,1,16,256]{3,2,1,0:T(8,128)S(1)}, f32[2,1,16,256]{3,2,1,0:T(8,128)S(1)}, u32[]{:S(2)}, u32[]{:S(2)}) collective-permute-start(f32[2,1,16,256]{3,2,1,0:T(8,128)S(1)} %get-tuple-element.59), channel_id=1, source_target_pairs={{0,4},{4,8},{8,12},{12,16},{16,20},{20,24},{24,28},{1,5},{5,9},{9,... | collective-permute-start | bytes 98312 | tf_op jit(solution)/shard_map/ppermute | solution.py:17
  82.6 5.2 %collective-permute-start.9 = (f32[2,1,16,256]{3,2,1,0:T(8,128)S(1)}, f32[2,1,16,256]{3,2,1,0:T(8,128)S(1)}, u32[]{:S(2)}, u32[]{:S(2)}) collective-permute-start(f32[2,1,16,256]{3,2,1,0:T(8,128)S(1)} %get-tuple-element.60), channel_id=1, source_target_pairs={{4,0},{8,4},{12,8},{16,12},{20,16},{24,20},{28,24},{5,1},{9,5},{13... | collective-permute-start | bytes 98312 | tf_op jit(solution)/shard_map/ppermute | solution.py:19
  87.8 7.0 %collective-permute-start.11 = (f32[2,10,1,256]{3,2,1,0:T(1,128)S(1)}, f32[2,10,1,256]{3,2,1,0:T(1,128)S(1)}, u32[]{:S(2)}, u32[]{:S(2)}) collective-permute-start(f32[2,10,1,256]{3,2,1,0:T(1,128)S(1)} %get-tuple-element.43), channel_id=1, source_target_pairs={{1,0},{2,1},{3,2},{5,4},{6,5},{7,6},{9,8},{10,9},{11,10},{13,12},{... | collective-permute-start | bytes 61448 | tf_op jit(solution)/shard_map/ppermute | solution.py:19
  90.1 5.6 %collective-permute-start.12 = (f32[2,10,1,256]{3,2,1,0:T(1,128)S(1)}, f32[2,10,1,256]{3,2,1,0:T(1,128)S(1)}, u32[]{:S(2)}, u32[]{:S(2)}) collective-permute-start(f32[2,10,1,256]{3,2,1,0:T(1,128)S(1)} %get-tuple-element.44), channel_id=1, source_target_pairs={{0,1},{1,2},{2,3},{4,5},{5,6},{6,7},{8,9},{9,10},{10,11},{12,13},{... | collective-permute-start | bytes 61448 | tf_op jit(solution)/shard_map/ppermute | solution.py:17
  96.1 3.9 %collective-permute-start.14 = (f32[2,1,16,256]{3,2,1,0:T(8,128)S(1)}, f32[2,1,16,256]{3,2,1,0:T(8,128)S(1)}, u32[]{:S(2)}, u32[]{:S(2)}) collective-permute-start(f32[2,1,16,256]{3,2,1,0:T(8,128)S(1)} %get-tuple-element.57), channel_id=1, source_target_pairs={{0,4},{4,8},{8,12},{12,16},{16,20},{20,24},{24,28},{1,5},{5,9},{9,... | collective-permute-start | bytes 98312 | tf_op jit(solution)/shard_map/ppermute | solution.py:17
  98.6 4.7 %collective-permute-start.13 = (f32[2,1,16,256]{3,2,1,0:T(8,128)S(1)}, f32[2,1,16,256]{3,2,1,0:T(8,128)S(1)}, u32[]{:S(2)}, u32[]{:S(2)}) collective-permute-start(f32[2,1,16,256]{3,2,1,0:T(8,128)S(1)} %get-tuple-element.58), channel_id=1, source_target_pairs={{4,0},{8,4},{12,8},{16,12},{20,16},{24,20},{28,24},{5,1},{9,5},{13... | collective-permute-start | bytes 98312 | tf_op jit(solution)/shard_map/ppermute | solution.py:19
  103.3 7.6 %collective-permute-start.15 = (f32[2,10,1,256]{3,2,1,0:T(1,128)S(1)}, f32[2,10,1,256]{3,2,1,0:T(1,128)S(1)}, u32[]{:S(2)}, u32[]{:S(2)}) collective-permute-start(f32[2,10,1,256]{3,2,1,0:T(1,128)S(1)} %get-tuple-element.41), channel_id=1, source_target_pairs={{1,0},{2,1},{3,2},{5,4},{6,5},{7,6},{9,8},{10,9},{11,10},{13,12},{... | collective-permute-start | bytes 61448 | tf_op jit(solution)/shard_map/ppermute | solution.py:19
  105.2 6.5 %collective-permute-start.16 = (f32[2,10,1,256]{3,2,1,0:T(1,128)S(1)}, f32[2,10,1,256]{3,2,1,0:T(1,128)S(1)}, u32[]{:S(2)}, u32[]{:S(2)}) collective-permute-start(f32[2,10,1,256]{3,2,1,0:T(1,128)S(1)} %get-tuple-element.42), channel_id=1, source_target_pairs={{0,1},{1,2},{2,3},{4,5},{5,6},{6,7},{8,9},{9,10},{10,11},{12,13},{... | collective-permute-start | bytes 61448 | tf_op jit(solution)/shard_map/ppermute | solution.py:17
  112.1 4.8 %collective-permute-start.18 = (f32[2,1,16,256]{3,2,1,0:T(8,128)S(1)}, f32[2,1,16,256]{3,2,1,0:T(8,128)S(1)}, u32[]{:S(2)}, u32[]{:S(2)}) collective-permute-start(f32[2,1,16,256]{3,2,1,0:T(8,128)S(1)} %get-tuple-element.55), channel_id=1, source_target_pairs={{0,4},{4,8},{8,12},{12,16},{16,20},{20,24},{24,28},{1,5},{5,9},{9,... | collective-permute-start | bytes 98312 | tf_op jit(solution)/shard_map/ppermute | solution.py:17
  115.6 4.7 %collective-permute-start.17 = (f32[2,1,16,256]{3,2,1,0:T(8,128)S(1)}, f32[2,1,16,256]{3,2,1,0:T(8,128)S(1)}, u32[]{:S(2)}, u32[]{:S(2)}) collective-permute-start(f32[2,1,16,256]{3,2,1,0:T(8,128)S(1)} %get-tuple-element.56), channel_id=1, source_target_pairs={{4,0},{8,4},{12,8},{16,12},{20,16},{24,20},{28,24},{5,1},{9,5},{13... | collective-permute-start | bytes 98312 | tf_op jit(solution)/shard_map/ppermute | solution.py:19
  120.3 7.6 %collective-permute-start.19 = (f32[2,10,1,256]{3,2,1,0:T(1,128)S(1)}, f32[2,10,1,256]{3,2,1,0:T(1,128)S(1)}, u32[]{:S(2)}, u32[]{:S(2)}) collective-permute-start(f32[2,10,1,256]{3,2,1,0:T(1,128)S(1)} %get-tuple-element.39), channel_id=1, source_target_pairs={{1,0},{2,1},{3,2},{5,4},{6,5},{7,6},{9,8},{10,9},{11,10},{13,12},{... | collective-permute-start | bytes 61448 | tf_op jit(solution)/shard_map/ppermute | solution.py:19
  122.2 6.5 %collective-permute-start.20 = (f32[2,10,1,256]{3,2,1,0:T(1,128)S(1)}, f32[2,10,1,256]{3,2,1,0:T(1,128)S(1)}, u32[]{:S(2)}, u32[]{:S(2)}) collective-permute-start(f32[2,10,1,256]{3,2,1,0:T(1,128)S(1)} %get-tuple-element.40), channel_id=1, source_target_pairs={{0,1},{1,2},{2,3},{4,5},{5,6},{6,7},{8,9},{9,10},{10,11},{12,13},{... | collective-permute-start | bytes 61448 | tf_op jit(solution)/shard_map/ppermute | solution.py:17
  129.1 5.2 %collective-permute-start.22 = (f32[2,1,16,256]{3,2,1,0:T(8,128)S(1)}, f32[2,1,16,256]{3,2,1,0:T(8,128)S(1)}, u32[]{:S(2)}, u32[]{:S(2)}) collective-permute-start(f32[2,1,16,256]{3,2,1,0:T(8,128)S(1)} %get-tuple-element.53), channel_id=1, source_target_pairs={{0,4},{4,8},{8,12},{12,16},{16,20},{20,24},{24,28},{1,5},{5,9},{9,... | collective-permute-start | bytes 98312 | tf_op jit(solution)/shard_map/ppermute | solution.py:17
  133.0 4.9 %collective-permute-start.21 = (f32[2,1,16,256]{3,2,1,0:T(8,128)S(1)}, f32[2,1,16,256]{3,2,1,0:T(8,128)S(1)}, u32[]{:S(2)}, u32[]{:S(2)}) collective-permute-start(f32[2,1,16,256]{3,2,1,0:T(8,128)S(1)} %get-tuple-element.54), channel_id=1, source_target_pairs={{4,0},{8,4},{12,8},{16,12},{20,16},{24,20},{28,24},{5,1},{9,5},{13... | collective-permute-start | bytes 98312 | tf_op jit(solution)/shard_map/ppermute | solution.py:19
  138.0 7.3 %collective-permute-start.23 = (f32[2,10,1,256]{3,2,1,0:T(1,128)S(1)}, f32[2,10,1,256]{3,2,1,0:T(1,128)S(1)}, u32[]{:S(2)}, u32[]{:S(2)}) collective-permute-start(f32[2,10,1,256]{3,2,1,0:T(1,128)S(1)} %get-tuple-element.37), channel_id=1, source_target_pairs={{1,0},{2,1},{3,2},{5,4},{6,5},{7,6},{9,8},{10,9},{11,10},{13,12},{... | collective-permute-start | bytes 61448 | tf_op jit(solution)/shard_map/ppermute | solution.py:19
  139.9 6.3 %collective-permute-start.24 = (f32[2,10,1,256]{3,2,1,0:T(1,128)S(1)}, f32[2,10,1,256]{3,2,1,0:T(1,128)S(1)}, u32[]{:S(2)}, u32[]{:S(2)}) collective-permute-start(f32[2,10,1,256]{3,2,1,0:T(1,128)S(1)} %get-tuple-element.38), channel_id=1, source_target_pairs={{0,1},{1,2},{2,3},{4,5},{5,6},{6,7},{8,9},{9,10},{10,11},{12,13},{... | collective-permute-start | bytes 61448 | tf_op jit(solution)/shard_map/ppermute | solution.py:17
  146.5 5.8 %collective-permute-start.26 = (f32[2,1,16,256]{3,2,1,0:T(8,128)S(1)}, f32[2,1,16,256]{3,2,1,0:T(8,128)S(1)}, u32[]{:S(2)}, u32[]{:S(2)}) collective-permute-start(f32[2,1,16,256]{3,2,1,0:T(8,128)S(1)} %get-tuple-element.51), channel_id=1, source_target_pairs={{0,4},{4,8},{8,12},{12,16},{16,20},{20,24},{24,28},{1,5},{5,9},{9,... | collective-permute-start | bytes 98312 | tf_op jit(solution)/shard_map/ppermute | solution.py:17
  151.1 4.7 %collective-permute-start.25 = (f32[2,1,16,256]{3,2,1,0:T(8,128)S(1)}, f32[2,1,16,256]{3,2,1,0:T(8,128)S(1)}, u32[]{:S(2)}, u32[]{:S(2)}) collective-permute-start(f32[2,1,16,256]{3,2,1,0:T(8,128)S(1)} %get-tuple-element.52), channel_id=1, source_target_pairs={{4,0},{8,4},{12,8},{16,12},{20,16},{24,20},{28,24},{5,1},{9,5},{13... | collective-permute-start | bytes 98312 | tf_op jit(solution)/shard_map/ppermute | solution.py:19
  155.8 7.6 %collective-permute-start.27 = (f32[2,10,1,256]{3,2,1,0:T(1,128)S(1)}, f32[2,10,1,256]{3,2,1,0:T(1,128)S(1)}, u32[]{:S(2)}, u32[]{:S(2)}) collective-permute-start(f32[2,10,1,256]{3,2,1,0:T(1,128)S(1)} %get-tuple-element.35), channel_id=1, source_target_pairs={{1,0},{2,1},{3,2},{5,4},{6,5},{7,6},{9,8},{10,9},{11,10},{13,12},{... | collective-permute-start | bytes 61448 | tf_op jit(solution)/shard_map/ppermute | solution.py:19
  157.7 6.5 %collective-permute-start.28 = (f32[2,10,1,256]{3,2,1,0:T(1,128)S(1)}, f32[2,10,1,256]{3,2,1,0:T(1,128)S(1)}, u32[]{:S(2)}, u32[]{:S(2)}) collective-permute-start(f32[2,10,1,256]{3,2,1,0:T(1,128)S(1)} %get-tuple-element.36), channel_id=1, source_target_pairs={{0,1},{1,2},{2,3},{4,5},{5,6},{6,7},{8,9},{9,10},{10,11},{12,13},{... | collective-permute-start | bytes 61448 | tf_op jit(solution)/shard_map/ppermute | solution.py:17
  164.6 4.3 %collective-permute-start.30 = (f32[2,1,16,256]{3,2,1,0:T(8,128)S(1)}, f32[2,1,16,256]{3,2,1,0:T(8,128)S(1)}, u32[]{:S(2)}, u32[]{:S(2)}) collective-permute-start(f32[2,1,16,256]{3,2,1,0:T(8,128)S(1)} %get-tuple-element.49), channel_id=1, source_target_pairs={{0,4},{4,8},{8,12},{12,16},{16,20},{20,24},{24,28},{1,5},{5,9},{9,... | collective-permute-start | bytes 98312 | tf_op jit(solution)/shard_map/ppermute | solution.py:17
  167.6 4.7 %collective-permute-start.29 = (f32[2,1,16,256]{3,2,1,0:T(8,128)S(1)}, f32[2,1,16,256]{3,2,1,0:T(8,128)S(1)}, u32[]{:S(2)}, u32[]{:S(2)}) collective-permute-start(f32[2,1,16,256]{3,2,1,0:T(8,128)S(1)} %get-tuple-element.50), channel_id=1, source_target_pairs={{4,0},{8,4},{12,8},{16,12},{20,16},{24,20},{28,24},{5,1},{9,5},{13... | collective-permute-start | bytes 98312 | tf_op jit(solution)/shard_map/ppermute | solution.py:19
  172.2 7.6 %collective-permute-start.31 = (f32[2,10,1,256]{3,2,1,0:T(1,128)S(1)}, f32[2,10,1,256]{3,2,1,0:T(1,128)S(1)}, u32[]{:S(2)}, u32[]{:S(2)}) collective-permute-start(f32[2,10,1,256]{3,2,1,0:T(1,128)S(1)} %get-tuple-element.33), channel_id=1, source_target_pairs={{1,0},{2,1},{3,2},{5,4},{6,5},{7,6},{9,8},{10,9},{11,10},{13,12},{... | collective-permute-start | bytes 61448 | tf_op jit(solution)/shard_map/ppermute | solution.py:19
  174.2 6.5 %collective-permute-start.32 = (f32[2,10,1,256]{3,2,1,0:T(1,128)S(1)}, f32[2,10,1,256]{3,2,1,0:T(1,128)S(1)}, u32[]{:S(2)}, u32[]{:S(2)}) collective-permute-start(f32[2,10,1,256]{3,2,1,0:T(1,128)S(1)} %get-tuple-element.34), channel_id=1, source_target_pairs={{0,1},{1,2},{2,3},{4,5},{5,6},{6,7},{8,9},{9,10},{10,11},{12,13},{... | collective-permute-start | bytes 61448 | tf_op jit(solution)/shard_map/ppermute | solution.py:17
  181.2 3.9 %collective-permute-start.34 = (f32[2,1,16,256]{3,2,1,0:T(8,128)S(1)}, f32[2,1,16,256]{3,2,1,0:T(8,128)S(1)}, u32[]{:S(2)}, u32[]{:S(2)}) collective-permute-start(f32[2,1,16,256]{3,2,1,0:T(8,128)S(1)} %get-tuple-element.47), channel_id=1, source_target_pairs={{0,4},{4,8},{8,12},{12,16},{16,20},{20,24},{24,28},{1,5},{5,9},{9,... | collective-permute-start | bytes 98312 | tf_op jit(solution)/shard_map/ppermute | solution.py:17
  183.8 4.7 %collective-permute-start.33 = (f32[2,1,16,256]{3,2,1,0:T(8,128)S(1)}, f32[2,1,16,256]{3,2,1,0:T(8,128)S(1)}, u32[]{:S(2)}, u32[]{:S(2)}) collective-permute-start(f32[2,1,16,256]{3,2,1,0:T(8,128)S(1)} %get-tuple-element.48), channel_id=1, source_target_pairs={{4,0},{8,4},{12,8},{16,12},{20,16},{24,20},{28,24},{5,1},{9,5},{13... | collective-permute-start | bytes 98312 | tf_op jit(solution)/shard_map/ppermute | solution.py:19
  188.5 8.3 %collective-permute-start.35 = (f32[2,10,1,256]{3,2,1,0:T(1,128)S(1)}, f32[2,10,1,256]{3,2,1,0:T(1,128)S(1)}, u32[]{:S(2)}, u32[]{:S(2)}) collective-permute-start(f32[2,10,1,256]{3,2,1,0:T(1,128)S(1)} %get-tuple-element.31), channel_id=1, source_target_pairs={{1,0},{2,1},{3,2},{5,4},{6,5},{7,6},{9,8},{10,9},{11,10},{13,12},{... | collective-permute-start | bytes 61448 | tf_op jit(solution)/shard_map/ppermute | solution.py:19
  190.4 6.5 %collective-permute-start.36 = (f32[2,10,1,256]{3,2,1,0:T(1,128)S(1)}, f32[2,10,1,256]{3,2,1,0:T(1,128)S(1)}, u32[]{:S(2)}, u32[]{:S(2)}) collective-permute-start(f32[2,10,1,256]{3,2,1,0:T(1,128)S(1)} %get-tuple-element.32), channel_id=1, source_target_pairs={{0,1},{1,2},{2,3},{4,5},{5,6},{6,7},{8,9},{9,10},{10,11},{12,13},{... | collective-permute-start | bytes 61448 | tf_op jit(solution)/shard_map/ppermute | solution.py:17
where the time goes:
time: 199 us; the launch traced here: 198 us
  starting transfers between devices  106 us (53%)
  waiting for transfers between devices  41.2 us (21%)
  blocking collectives  40.9 us (21%)
  other arithmetic  7.13 us (4%)
    ppermute x16, starting transfers between devices, padded_2(): lax.ppermute(tail, axis, [(i, (i + 1) % count) for i in range(ends)])  65.2 us
    pmax x1, blocking collectives, shards(): lax.pmax(jnp.max(shift + 2.0 * (coef_x + low_x + coef_y + low_y + coef_z...  40.9 us
    ppermute x16, starting transfers between devices, padded_2(): lax.ppermute(head, axis, [((i + 1) % count, i) for i in range(ends)])  29.9 us
    ppermute x16, waiting for transfers between devices, padded_2(): lax.ppermute(head, axis, [((i + 1) % count, i) for i in range(ends)])  27.6 us
    ppermute x3, waiting for transfers between devices, from_partner(): lax.ppermute(array, axis, [(i, i ^ 1 << apart) for i in range(lax.axis_si...  7.34 us
    ppermute x2, starting transfers between devices, passed_along(): return lax.ppermute(array, axis, pairs)  6.68 us
    ppermute x16, waiting for transfers between devices, padded_2(): lax.ppermute(tail, axis, [(i, (i + 1) % count) for i in range(ends)])  6.34 us
  transfers between devices with their start and end apart: 37, of which 17 were waited for; matrix products, arithmetic and copies ran while one was open for 2% of the time, Pallas kernels for 0%

commit v1 on v0

v1 whole, which is shorter than its diff:
```python
import functools

import jax
import jax.numpy as jnp
from jax import lax
from jax.experimental import pallas as pl
from jax.experimental.pallas import tpu as pltpu
from jax.sharding import PartitionSpec as P

ITERS = 8
MESH = pl.DeviceIdType.MESH


def kernel(nx, ny, low_ref, high_ref, b_ref, sh_ref, cx_ref, cy_ref, cz_ref, p_ref, q_ref,
           D, HX, HY, FY, M, LXH, LYH, SY, LY, LZ, CZ, DG, R, XS, G1, G2, L1, L2,
           send_h, recv_h, send_c, recv_c, send_1, recv_1, send_2, recv_2):
    X, Y, Z = b_ref.shape
    ix, iy = lax.axis_index("gx"), lax.axis_index("gy")
    inner = (ix > 0, ix < nx - 1, iy > 0, iy < ny - 1)

    @pl.when(ix == 0)
    def _():
        HX[:, 0] = jnp.zeros_like(HX[:, 0])
        LXH[...] = jnp.zeros_like(LXH)

    @pl.when(ix == nx - 1)
    def _():
        HX[:, 1] = jnp.zeros_like(HX[:, 1])

    @pl.when(iy == 0)
    def _():
        HY[:, 0] = jnp.zeros_like(HY[:, 0])
        LYH[...] = jnp.zeros_like(LYH)

    @pl.when(iy == ny - 1)
    def _():
        HY[:, 1] = jnp.zeros_like(HY[:, 1])

    for x in range(X):
        SY[pl.ds(x, 1), :] = cy_ref[x, Y - 1:Y, :]

    barrier = pltpu.get_barrier_semaphore()
    for o in range(1, nx):
        pl.semaphore_signal(barrier, inc=1, device_id=(lax.rem(ix + o, nx), iy), device_id_type=MESH)
    for o in range(1, ny):
        pl.semaphore_signal(barrier, inc=1, device_id=(ix, lax.rem(iy + o, ny)), device_id_type=MESH)
    pl.semaphore_wait(barrier, nx + ny - 2)

    def remote(src, dst, send, recv, to):
        return pltpu.make_async_remote_copy(
            src_ref=src, dst_ref=dst, send_sem=send, recv_sem=recv, device_id=to, device_id_type=MESH)

    to_up_x = (lax.rem(ix + 1, nx), iy)
    to_dn_x = (lax.rem(ix + nx - 1, nx), iy)
    to_up_y = (ix, lax.rem(iy + 1, ny))
    to_dn_y = (ix, lax.rem(iy + ny - 1, ny))

    mirror = remote(b_ref, M, send_c.at[2], recv_c.at[2], (nx - 1 - ix, iy))
    coef_x = remote(cx_ref.at[X - 1], LXH, send_c.at[0], recv_c.at[0], to_up_x)
    coef_y = remote(SY, LYH, send_c.at[1], recv_c.at[1], to_up_y)
    pl.when(inner[1])(coef_x.start)
    pl.when(inner[3])(coef_y.start)
    mirror.start()

    def copies(s):
        return (
            (remote(D.at[s, X - 1], HX.at[s, 0], send_h.at[s, 0], recv_h.at[s, 0], to_up_x), inner[1], inner[0]),
            (remote(D.at[s, 0], HX.at[s, 1], send_h.at[s, 1], recv_h.at[s, 1], to_dn_x), inner[0], inner[1]),
            (remote(FY.at[s, 1], HY.at[s, 0], send_h.at[s, 2], recv_h.at[s, 2], to_up_y), inner[3], inner[2]),
            (remote(FY.at[s, 0], HY.at[s, 1], send_h.at[s, 3], recv_h.at[s, 3], to_dn_y), inner[2], inner[3]),
        )

    def start(s):
        for copy, sends, _ in copies(s):
            pl.when(sends)(copy.start)

    def arrive(s):
        for copy, _, receives in copies(s):
            pl.when(receives)(copy.wait_recv)

    def put(s, x, v):
        D[s, x] = v
        FY[s, 0, :, pl.ds(x, 1), :] = v[:, 0:1, :]
        FY[s, 1, :, pl.ds(x, 1), :] = v[:, Y - 1:Y, :]

    row = lax.broadcasted_iota(jnp.int32, (2, Y, Z), 1)

    def apply(s, x):
        v = D[s, x]
        up = D[s, x + 1] if x < X - 1 else HX[s, 1]
        dn = D[s, x - 1] if x > 0 else HX[s, 0]
        lx = cx_ref[x - 1] if x > 0 else LXH[...]
        yu = jnp.where(row == Y - 1, HY[s, 1, :, pl.ds(x, 1), :], pltpu.roll(v, Y - 1, 1))
        yd = jnp.where(row == 0, HY[s, 0, :, pl.ds(x, 1), :], pltpu.roll(v, 1, 1))
        zu, zd = pltpu.roll(v, Z - 1, 2), pltpu.roll(v, 1, 2)
        t = DG[x][None] * v - cx_ref[x][None] * up - lx[None] * dn
        t = t - cy_ref[x][None] * yu - LY[x][None] * yd
        return t - CZ[x][None] * zu - LZ[x][None] * zd

    pl.when(inner[0])(coef_x.wait_recv)
    pl.when(inner[2])(coef_y.wait_recv)
    row1 = lax.broadcasted_iota(jnp.int32, (Y, Z), 0)
    col1 = lax.broadcasted_iota(jnp.int32, (Y, Z), 1)
    top = None
    for x in range(X):
        cx, cy, cz, sh = cx_ref[x], cy_ref[x], cz_ref[x], sh_ref[x]
        lx = cx_ref[x - 1] if x > 0 else LXH[...]
        ly = jnp.where(row1 == 0, LYH[pl.ds(x, 1), :], pltpu.roll(cy, 1, 0))
        lz = jnp.where(col1 == 0, 0.0, pltpu.roll(cz, 1, 1))
        around = cx + lx + cy + ly + cz + lz
        LY[x] = ly
        LZ[x] = lz
        CZ[x] = jnp.where(col1 == Z - 1, 0.0, cz)
        DG[x] = sh + around
        here = sh + 2.0 * around
        top = here if top is None else jnp.maximum(top, here)
    tile = None
    for y in range(0, Y, 8):
        for z in range(0, Z, 128):
            part = top[y:y + 8, z:z + 128]
            tile = part if tile is None else jnp.maximum(tile, part)
    L1[...] = tile

    first = [remote(L1, G1.at[o - 1], send_1.at[o - 1], recv_1.at[o - 1], (ix, lax.rem(iy + o, ny)))
             for o in range(1, ny)]
    second = [remote(L2, G2.at[o - 1], send_2.at[o - 1], recv_2.at[o - 1], (lax.rem(ix + o, nx), iy))
              for o in range(1, nx)]
    for copy in first:
        copy.start()

    mirror.wait_recv()
    for x in range(X):
        b, m = b_ref[x], M[X - 1 - x]
        put(0, x, jnp.stack([(b + m) / 2.0, (b - m) / 2.0]))
    start(0)

    tile = L1[...]
    for o, copy in enumerate(first):
        copy.wait_recv()
        tile = jnp.maximum(tile, G1[o])
    L2[...] = tile
    for copy in second:
        copy.start()

    arrive(0)
    for x in range(X):
        put(1, x, apply(0, x))
    start(1)

    tile = L2[...]
    for o, copy in enumerate(second):
        copy.wait_recv()
        tile = jnp.maximum(tile, G2[o])
    bound = jnp.max(jnp.max(tile, axis=0, keepdims=True), axis=1, keepdims=True)
    bound = jnp.broadcast_to(bound[None], (2, 1, Z))
    which = lax.broadcasted_iota(jnp.int32, (2, 1, Z), 0)
    lmin = jnp.where(which == 0, low_ref[0], low_ref[1]) * bound
    lmax = jnp.where(which == 0, high_ref[0], high_ref[1]) * bound
    theta = (lmax + lmin) / 2.0
    delta = (lmax - lmin) / 2.0
    sigma = theta / delta
    rho0 = 1.0 / sigma
    rho1 = 1.0 / (2.0 * sigma - rho0)
    rho2 = 1.0 / (2.0 * sigma - rho1)
    inv = 1.0 / theta
    g1, g2 = 2.0 * rho1 / delta, 2.0 * rho2 / delta
    alpha, beta = rho1 * rho0 * inv + g1, -g1 * inv

    arrive(1)
    for x in range(X):
        w2 = apply(1, x)
        r0, w1 = D[0, x], D[1, x]
        d1 = r0 * inv
        d2 = alpha * r0 + beta * w1
        r2 = (r0 - inv * w1) - (alpha * w1 + beta * w2)
        d3 = rho2 * rho1 * d2 + g2 * r2
        R[x] = r2
        XS[x] = d1 + d2 + d3
        put(2, x, d3)
    start(2)

    def step(s, rho):
        rho_new = 1.0 / (2.0 * sigma - rho)
        a, g = rho_new * rho, 2.0 * rho_new / delta
        arrive(s)
        for x in range(X):
            r = R[x] - apply(s, x)
            d = a * D[s, x] + g * r
            R[x] = r
            XS[x] = XS[x] + d
            put(s + 1, x, d)
        start(s + 1)
        return rho_new

    lax.fori_loop(2, ITERS - 1, step, rho2)

    arrive(ITERS - 1)
    for x in range(X):
        r = R[x] - apply(ITERS - 1, x)
        q_ref[x] = r[0] + r[1]
        xs = XS[x]
        p_ref[x] = xs[0] + xs[1]

    def drain(s, carry):
        for copy, sends, _ in copies(s):
            pl.when(sends)(copy.wait_send)
        return carry

    lax.fori_loop(0, ITERS, drain, 0)
    mirror.wait_send()
    pl.when(inner[1])(coef_x.wait_send)
    pl.when(inner[3])(coef_y.wait_send)
    for copy in first + second:
        copy.wait_send()


def solution(mesh):
    nx, ny = mesh.shape["gx"], mesh.shape["gy"]

    def shards(right_side, shift, coef_x, coef_y, coef_z, low_frac, high_frac):
        X, Y, Z = right_side.shape
        f32 = jnp.float32
        S = ITERS
        vmem = pl.BlockSpec(memory_space=pltpu.VMEM)
        smem = pl.BlockSpec(memory_space=pltpu.SMEM)
        block = jax.ShapeDtypeStruct((X, Y, Z), f32)
        dma = pltpu.SemaphoreType.DMA
        cells = pltpu.VMEM((X, Y, Z), f32)
        return pl.pallas_call(
            functools.partial(kernel, nx, ny),
            out_shape=(block, block),
            in_specs=[smem, smem] + [vmem] * 5,
            out_specs=(vmem, vmem),
            scratch_shapes=[
                pltpu.VMEM((S, X, 2, Y, Z), f32),
                pltpu.VMEM((S, 2, 2, Y, Z), f32),
                pltpu.VMEM((S, 2, 2, X, Z), f32),
                pltpu.VMEM((S, 2, 2, X, Z), f32),
                cells,
                pltpu.VMEM((Y, Z), f32),
                pltpu.VMEM((X, Z), f32),
                pltpu.VMEM((X, Z), f32),
                cells, cells, cells, cells,
                pltpu.VMEM((X, 2, Y, Z), f32),
                pltpu.VMEM((X, 2, Y, Z), f32),
                pltpu.VMEM((ny - 1, 8, 128), f32),
                pltpu.VMEM((nx - 1, 8, 128), f32),
                pltpu.VMEM((8, 128), f32),
                pltpu.VMEM((8, 128), f32),
                dma((S, 4)), dma((S, 4)),
                dma((3,)), dma((3,)),
                dma((ny - 1,)), dma((ny - 1,)),
                dma((nx - 1,)), dma((nx - 1,)),
            ],
            compiler_params=pltpu.CompilerParams(
                collective_id=0, has_side_effects=True, vmem_limit_bytes=16 * 1024 * 1024),
        )(low_frac, high_frac, right_side, shift, coef_x, coef_y, coef_z)

    block = P("gx", "gy", None)
    return jax.shard_map(
        shards,
        mesh=mesh,
        in_specs=(block,) * 5 + (P(), P()),
        out_specs=(block, block),
        check_vma=False,
    )
```

time: 199 us -> 51.2 us (0.26)
  the two profiles are of different devices: /device:TPU:1 before, /device:TPU:0 now
where the time goes in v1:
time: 51.2 us; the launch traced here: 51 us
  Pallas kernels  43.2 us (84%)
  local copies, waits for them, and re-layouts  7.13 us (14%)
  between operations  0.66 us (1%)
    pallas_call x1, Pallas kernels, shards(): pl.pallas_call(functools.partial(kernel, nx, ny), out_shape=(block, block...  43.2 us
    unnamed x16, local copies, waits for them, and re-layouts  7.13 us

profile of v1, /device:TPU:0, one launch (start us, length us, event | category | flops | bytes accessed | tf_op | source)
XLA Modules:
  0.0 51.0 jit_solution(4910434670418926)
XLA Ops:
  0.6 0.0 copy-start
  0.6 0.9 %copy-done = f32[8,16,256]{2,1,0:T(8,128)S(1)} copy-done((f32[8,16,256]{2,1,0:T(8,128)S(1)}, f32[8,16,256]{2,1,0:T(8,128)}, u32[]{:S(2)}) %copy-start) | copy-done | bytes 131096
  1.5 0.0 copy-start.1
  1.5 0.9 %copy-done.1 = f32[8,16,256]{2,1,0:T(8,128)S(1)} copy-done((f32[8,16,256]{2,1,0:T(8,128)S(1)}, f32[8,16,256]{2,1,0:T(8,128)}, u32[]{:S(2)}) %copy-start.1) | copy-done | bytes 131096
  2.4 0.0 copy-start.2
  2.4 0.9 %copy-done.2 = f32[8,16,256]{2,1,0:T(8,128)S(1)} copy-done((f32[8,16,256]{2,1,0:T(8,128)S(1)}, f32[8,16,256]{2,1,0:T(8,128)}, u32[]{:S(2)}) %copy-start.2) | copy-done | bytes 131096
  3.3 0.0 copy-start.3
  3.3 0.9 %copy-done.3 = f32[8,16,256]{2,1,0:T(8,128)S(1)} copy-done((f32[8,16,256]{2,1,0:T(8,128)S(1)}, f32[8,16,256]{2,1,0:T(8,128)}, u32[]{:S(2)}) %copy-start.3) | copy-done | bytes 131096
  4.3 0.0 copy-start.4
  4.3 0.9 %copy-done.4 = f32[8,16,256]{2,1,0:T(8,128)S(1)} copy-done((f32[8,16,256]{2,1,0:T(8,128)S(1)}, f32[8,16,256]{2,1,0:T(8,128)}, u32[]{:S(2)}) %copy-start.4) | copy-done | bytes 131096
  5.2 0.0 copy-start.5
  5.2 0.7 %copy-done.5 = f32[2]{0:T(128)S(1)} copy-done((f32[2]{0:T(128)S(1)}, f32[2]{0:T(128)}, u32[]{:S(2)}) %copy-start.5) | copy-done | bytes 32
  5.8 0.0 copy-start.6
  5.8 0.7 %copy-done.6 = f32[2]{0:T(128)S(1)} copy-done((f32[2]{0:T(128)S(1)}, f32[2]{0:T(128)}, u32[]{:S(2)}) %copy-start.6) | copy-done | bytes 32
  6.5 43.2 %shard_map.86 = (f32[8,16,256]{2,1,0:T(8,128)S(1)}, f32[8,16,256]{2,1,0:T(8,128)S(1)}) custom-call(f32[2]{0:T(128)S(1)} %copy-done.5, f32[2]{0:T(128)S(1)} %copy-done.6, f32[8,16,256]{2,1,0:T(8,128)S(1)} %copy-done, f32[8,16,256]{2,1,0:T(8,128)S(1)} %copy-done.1, f32[8,16,256]{2,1,0:T(8,128)S(1)} %copy-done.2, f32[8,16,256]{2,1,0:T(8,128)S(1)} %copy-done.3, ...), custom_call_target="tpu_custom_call" | custom-call | tf_op jit(solution)/shard_map/pallas_call | solution.py:229
  49.7 0.7 %copy.11 = f32[8,16,256]{2,1,0:T(8,128)} copy(f32[8,16,256]{2,1,0:T(8,128)S(1)} %get-tuple-element.4) | data formatting | bytes 262144
  50.4 0.7 %copy.12 = f32[8,16,256]{2,1,0:T(8,128)} copy(f32[8,16,256]{2,1,0:T(8,128)S(1)} %get-tuple-element.5) | data formatting | bytes 262144
Async XLA Ops:
  0.6 0.9 %copy-start = (f32[8,16,256]{2,1,0:T(8,128)S(1)}, f32[8,16,256]{2,1,0:T(8,128)}, u32[]{:S(2)}) copy-start(f32[8,16,256]{2,1,0:T(8,128)} %b_ref.1) | copy-start | bytes 393220
  1.5 0.9 %copy-start.1 = (f32[8,16,256]{2,1,0:T(8,128)S(1)}, f32[8,16,256]{2,1,0:T(8,128)}, u32[]{:S(2)}) copy-start(f32[8,16,256]{2,1,0:T(8,128)} %sh_ref.1) | copy-start | bytes 393220
  2.4 0.9 %copy-start.2 = (f32[8,16,256]{2,1,0:T(8,128)S(1)}, f32[8,16,256]{2,1,0:T(8,128)}, u32[]{:S(2)}) copy-start(f32[8,16,256]{2,1,0:T(8,128)} %cx_ref.1) | copy-start | bytes 393220
  3.3 0.9 %copy-start.3 = (f32[8,16,256]{2,1,0:T(8,128)S(1)}, f32[8,16,256]{2,1,0:T(8,128)}, u32[]{:S(2)}) copy-start(f32[8,16,256]{2,1,0:T(8,128)} %cy_ref.1) | copy-start | bytes 393220
  4.3 0.9 %copy-start.4 = (f32[8,16,256]{2,1,0:T(8,128)S(1)}, f32[8,16,256]{2,1,0:T(8,128)}, u32[]{:S(2)}) copy-start(f32[8,16,256]{2,1,0:T(8,128)} %cz_ref.1) | copy-start | bytes 393220
  5.2 0.7 %copy-start.5 = (f32[2]{0:T(128)S(1)}, f32[2]{0:T(128)}, u32[]{:S(2)}) copy-start(f32[2]{0:T(128)} %low_ref.1) | copy-start | bytes 28
  5.8 0.7 %copy-start.6 = (f32[2]{0:T(128)S(1)}, f32[2]{0:T(128)}, u32[]{:S(2)}) copy-start(f32[2]{0:T(128)} %high_ref.1) | copy-start | bytes 28

commit v2 on v1

--- a/solution.py
+++ b/solution.py
@@ -8,42 +8,52 @@
 from jax.sharding import PartitionSpec as P
 
 ITERS = 8
+HALF = 12.25
 MESH = pl.DeviceIdType.MESH
 
 
-def kernel(nx, ny, low_ref, high_ref, b_ref, sh_ref, cx_ref, cy_ref, cz_ref, p_ref, q_ref,
-           D, HX, HY, FY, M, LXH, LYH, SY, LY, LZ, CZ, DG, R, XS, G1, G2, L1, L2,
+def kernel(nx, ny, low_in, high_in, b_in, sh_in, cx_in, cy_in, cz_in, p_ref, q_ref,
+           low_ref, high_ref, b_ref, sh_ref, cx_ref, cy_ref, cz_ref, in_sem, CO,
+           D, HX, HY, FY, M, LXH, LYH, SY, LY, LZ, CZ, DG, G1, G2, L1, L2,
            send_h, recv_h, send_c, recv_c, send_1, recv_1, send_2, recv_2):
     X, Y, Z = b_ref.shape
     ix, iy = lax.axis_index("gx"), lax.axis_index("gy")
-    inner = (ix > 0, ix < nx - 1, iy > 0, iy < ny - 1)
-
-    @pl.when(ix == 0)
-    def _():
-        HX[:, 0] = jnp.zeros_like(HX[:, 0])
-        LXH[...] = jnp.zeros_like(LXH)
-
-    @pl.when(ix == nx - 1)
-    def _():
-        HX[:, 1] = jnp.zeros_like(HX[:, 1])
-
-    @pl.when(iy == 0)
-    def _():
-        HY[:, 0] = jnp.zeros_like(HY[:, 0])
-        LYH[...] = jnp.zeros_like(LYH)
-
-    @pl.when(iy == ny - 1)
-    def _():
-        HY[:, 1] = jnp.zeros_like(HY[:, 1])
-
-    for x in range(X):
-        SY[pl.ds(x, 1), :] = cy_ref[x, Y - 1:Y, :]
-
     barrier = pltpu.get_barrier_semaphore()
     for o in range(1, nx):
         pl.semaphore_signal(barrier, inc=1, device_id=(lax.rem(ix + o, nx), iy), device_id_type=MESH)
     for o in range(1, ny):
         pl.semaphore_signal(barrier, inc=1, device_id=(ix, lax.rem(iy + o, ny)), device_id_type=MESH)
+    pairs = ((cx_in, cx_ref), (cy_in, cy_ref), (b_in, b_ref), (cz_in, cz_ref), (sh_in, sh_ref),
+             (low_in, low_ref), (high_in, high_ref))
+    loads = [pltpu.make_async_copy(src, dst, in_sem.at[k]) for k, (src, dst) in enumerate(pairs)]
+    for load in loads:
+        load.start()
+
+    inner = (ix > 0, ix < nx - 1, iy > 0, iy < ny - 1)
+
+    @pl.when(ix == 0)
+    def _():
+        HX[:, 0] = jnp.zeros_like(HX[:, 0])
+        LXH[...] = jnp.zeros_like(LXH)
+
+    @pl.when(ix == nx - 1)
+    def _():
+        HX[:, 1] = jnp.zeros_like(HX[:, 1])
+
+    @pl.when(iy == 0)
+    def _():
+        HY[:, 0] = jnp.zeros_like(HY[:, 0])
+        LYH[...] = jnp.zeros_like(LYH)
+
+    @pl.when(iy == ny - 1)
+    def _():
+        HY[:, 1] = jnp.zeros_like(HY[:, 1])
+
+    loads[0].wait()
+    loads[1].wait()
+    for x in range(X):
+        SY[pl.ds(x, 1), :] = cy_ref[x, Y - 1:Y, :]
+    loads[2].wait()
     pl.semaphore_wait(barrier, nx + ny - 2)
 
     def remote(src, dst, send, recv, to):
@@ -74,9 +84,16 @@
         for copy, sends, _ in copies(s):
             pl.when(sends)(copy.start)
 
-    def arrive(s):
-        for copy, _, receives in copies(s):
+    def arrive(s, along):
+        for copy, _, receives in copies(s)[2 * along:2 * along + 2]:
             pl.when(receives)(copy.wait_recv)
+
+    def planes(s):
+        arrive(s, 1)
+        yield from range(1, X - 1)
+        arrive(s, 0)
+        yield 0
+        yield X - 1
 
     def put(s, x, v):
         D[s, x] = v
@@ -99,6 +116,8 @@
 
     pl.when(inner[0])(coef_x.wait_recv)
     pl.when(inner[2])(coef_y.wait_recv)
+    for load in loads[3:]:
+        load.wait()
     row1 = lax.broadcasted_iota(jnp.int32, (Y, Z), 0)
     col1 = lax.broadcasted_iota(jnp.int32, (Y, Z), 1)
     top = None
@@ -111,7 +130,7 @@
         LY[x] = ly
         LZ[x] = lz
         CZ[x] = jnp.where(col1 == Z - 1, 0.0, cz)
-        DG[x] = sh + around
+        DG[x] = (sh - HALF) + around
         here = sh + 2.0 * around
         top = here if top is None else jnp.maximum(top, here)
     tile = None
@@ -130,10 +149,20 @@
 
     mirror.wait_recv()
     for x in range(X):
-        b, m = b_ref[x], M[X - 1 - x]
-        put(0, x, jnp.stack([(b + m) / 2.0, (b - m) / 2.0]))
+        put(0, x, jnp.stack([b_ref[x], M[X - 1 - x]]))
     start(0)
 
+    for x in planes(0):
+        put(1, x, apply(0, x) * (1.0 / HALF))
+    start(1)
+
+    def step(s, carry):
+        for x in planes(s):
+            put(s + 1, x, apply(s, x) * (2.0 / HALF) - D[s - 1, x])
+        start(s + 1)
+        return carry
+
+    step(1, 0)
     tile = L1[...]
     for o, copy in enumerate(first):
         copy.wait_recv()
@@ -142,64 +171,52 @@
     for copy in second:
         copy.start()
 
-    arrive(0)
-    for x in range(X):
-        put(1, x, apply(0, x))
-    start(1)
+    lax.fori_loop(2, ITERS - 1, step, 0)
 
     tile = L2[...]
     for o, copy in enumerate(second):
         copy.wait_recv()
         tile = jnp.maximum(tile, G2[o])
     bound = jnp.max(jnp.max(tile, axis=0, keepdims=True), axis=1, keepdims=True)
-    bound = jnp.broadcast_to(bound[None], (2, 1, Z))
-    which = lax.broadcasted_iota(jnp.int32, (2, 1, Z), 0)
-    lmin = jnp.where(which == 0, low_ref[0], low_ref[1]) * bound
-    lmax = jnp.where(which == 0, high_ref[0], high_ref[1]) * bound
+
+    field = lax.broadcasted_iota(jnp.int32, (8, 128), 0)
+    lane = lax.broadcasted_iota(jnp.int32, (8, 128), 1)
+    lmin = jnp.where(field == 0, low_ref[0], low_ref[1]) * bound
+    lmax = jnp.where(field == 0, high_ref[0], high_ref[1]) * bound
     theta = (lmax + lmin) / 2.0
     delta = (lmax - lmin) / 2.0
     sigma = theta / delta
-    rho0 = 1.0 / sigma
-    rho1 = 1.0 / (2.0 * sigma - rho0)
-    rho2 = 1.0 / (2.0 * sigma - rho1)
-    inv = 1.0 / theta
-    g1, g2 = 2.0 * rho1 / delta, 2.0 * rho2 / delta
-    alpha, beta = rho1 * rho0 * inv + g1, -g1 * inv
-
-    arrive(1)
-    for x in range(X):
-        w2 = apply(1, x)
-        r0, w1 = D[0, x], D[1, x]
-        d1 = r0 * inv
-        d2 = alpha * r0 + beta * w1
-        r2 = (r0 - inv * w1) - (alpha * w1 + beta * w2)
-        d3 = rho2 * rho1 * d2 + g2 * r2
-        R[x] = r2
-        XS[x] = d1 + d2 + d3
-        put(2, x, d3)
-    start(2)
-
-    def step(s, rho):
+    rho = 1.0 / sigma
+    xs = jnp.zeros((8, 128), jnp.float32)
+    r = jnp.where(lane == 0, 1.0, xs)
+    d = r / theta
+    for _ in range(ITERS):
+        xs = xs + d
+        up = jnp.where(lane == 0, 0.0, pltpu.roll(d, 1, 1))
+        around = up + pltpu.roll(d, 127, 1) + jnp.where(lane == 1, up, 0.0)
+        r = r - HALF * (d + 0.5 * around)
         rho_new = 1.0 / (2.0 * sigma - rho)
-        a, g = rho_new * rho, 2.0 * rho_new / delta
-        arrive(s)
-        for x in range(X):
-            r = R[x] - apply(s, x)
-            d = a * D[s, x] + g * r
-            R[x] = r
-            XS[x] = XS[x] + d
-            put(s + 1, x, d)
-        start(s + 1)
-        return rho_new
-
-    lax.fori_loop(2, ITERS - 1, step, rho2)
-
-    arrive(ITERS - 1)
-    for x in range(X):
-        r = R[x] - apply(ITERS - 1, x)
-        q_ref[x] = r[0] + r[1]
-        xs = XS[x]
-        p_ref[x] = xs[0] + xs[1]
+        d = rho_new * rho * d + 2.0 * rho_new / delta * r
+        rho = rho_new
+    for j, c in enumerate((xs, r)):
+        both = (c[0:1] + c[1:2]) * 0.5, (c[0:1] - c[1:2]) * 0.5
+        for f in range(2):
+            for k in range(ITERS + 1):
+                CO[k, j, f] = jnp.broadcast_to(both[f][:, k:k + 1], (1, Z))
+
+    for x in range(X):
+        p = q = None
+        for k in range(ITERS):
+            for f in range(2):
+                w = D[k, x, f]
+                tp, tq = CO[k, 0, f] * w, CO[k, 1, f] * w
+                p, q = (tp, tq) if p is None else (p + tp, q + tq)
+        p_ref[x] = p
+        q_ref[x] = q
+    for x in planes(ITERS - 1):
+        w = apply(ITERS - 1, x) * (2.0 / HALF) - D[ITERS - 2, x]
+        p_ref[x] = p_ref[x] + CO[ITERS, 0, 0] * w[0] + CO[ITERS, 0, 1] * w[1]
+        q_ref[x] = q_ref[x] + CO[ITERS, 1, 0] * w[0] + CO[ITERS, 1, 1] * w[1]
 
     def drain(s, carry):
         for copy, sends, _ in copies(s):
@@ -222,16 +239,19 @@
         f32 = jnp.float32
         S = ITERS
         vmem = pl.BlockSpec(memory_space=pltpu.VMEM)
-        smem = pl.BlockSpec(memory_space=pltpu.SMEM)
         block = jax.ShapeDtypeStruct((X, Y, Z), f32)
         dma = pltpu.SemaphoreType.DMA
         cells = pltpu.VMEM((X, Y, Z), f32)
         return pl.pallas_call(
             functools.partial(kernel, nx, ny),
             out_shape=(block, block),
-            in_specs=[smem, smem] + [vmem] * 5,
+            in_specs=[pl.BlockSpec(memory_space=pl.ANY)] * 7,
             out_specs=(vmem, vmem),
             scratch_shapes=[
+                pltpu.SMEM((2,), f32), pltpu.SMEM((2,), f32),
+                cells, cells, cells, cells, cells,
+                dma((7,)),
+                pltpu.VMEM((S + 1, 2, 2, 1, Z), f32),
                 pltpu.VMEM((S, X, 2, Y, Z), f32),
                 pltpu.VMEM((S, 2, 2, Y, Z), f32),
                 pltpu.VMEM((S, 2, 2, X, Z), f32),
@@ -241,8 +261,6 @@
                 pltpu.VMEM((X, Z), f32),
                 pltpu.VMEM((X, Z), f32),
                 cells, cells, cells, cells,
-                pltpu.VMEM((X, 2, Y, Z), f32),
-                pltpu.VMEM((X, 2, Y, Z), f32),
                 pltpu.VMEM((ny - 1, 8, 128), f32),
                 pltpu.VMEM((nx - 1, 8, 128), f32),
                 pltpu.VMEM((8, 128), f32),
@@ -253,7 +271,7 @@
                 dma((nx - 1,)), dma((nx - 1,)),
             ],
             compiler_params=pltpu.CompilerParams(
-                collective_id=0, has_side_effects=True, vmem_limit_bytes=16 * 1024 * 1024),
+                collective_id=0, has_side_effects=True, vmem_limit_bytes=63488 * 1024),
         )(low_frac, high_frac, right_side, shift, coef_x, coef_y, coef_z)
 
     block = P("gx", "gy", None)

time: 51.2 us -> 45.4 us (0.89)
  local copies, waits for them, and re-layouts: 7.13 us -> 2.26 us
  Pallas kernels: 43.2 us -> 42.3 us
    unnamed x16 -> x4, local copies, waits for them, and re-layouts: 7.13 us -> 2.26 us
    pallas_call x1, Pallas kernels: 43.2 us -> 42.3 us  [shards(): pl.pallas_call(functools.partial(kernel, nx, ny), out_shape=(block, block...]
where the time goes in v2:
time: 45.4 us; the launch traced here: 45.2 us
  Pallas kernels  42.3 us (93%)
  local copies, waits for them, and re-layouts  2.26 us (5%)
  between operations  0.65 us (1%)
    pallas_call x1, Pallas kernels, shards(): pl.pallas_call(functools.partial(kernel, nx, ny), out_shape=(block, block...  42.3 us
    unnamed x4, local copies, waits for them, and re-layouts  2.26 us

profile of v2, /device:TPU:0, one launch (start us, length us, event | category | flops | bytes accessed | tf_op | source)
XLA Modules:
  0.0 45.2 jit_solution(4033733114176083293)
XLA Ops:
  0.6 42.3 %shard_map.86 = (f32[8,16,256]{2,1,0:T(8,128)}, f32[8,16,256]{2,1,0:T(8,128)}) custom-call(f32[2]{0:T(128)} %low_in.1, f32[2]{0:T(128)} %high_in.1, f32[8,16,256]{2,1,0:T(8,128)} %b_in.1, f32[8,16,256]{2,1,0:T(8,128)} %sh_in.1, f32[8,16,256]{2,1,0:T(8,128)} %cx_in.1, f32[8,16,256]{2,1,0:T(8,128)} %cy_in.1, f32[8,16,256]{2,1,0:T(8,128)} %cz_in.1), custom_call_target="tpu_custom_call" | custom-call | tf_op jit(solution)/shard_map/pallas_call | solution.py:245
  42.9 0.0 copy-start
  42.9 1.6 %copy.11 = f32[8,16,256]{2,1,0:T(8,128)} copy(f32[8,16,256]{2,1,0:T(8,128)} %get-tuple-element.4) | data formatting | bytes 262144
  44.5 0.0 copy-done
  44.5 0.7 %copy.12 = f32[8,16,256]{2,1,0:T(8,128)} copy(f32[8,16,256]{2,1,0:T(8,128)S(1)} %copy-done) | data formatting | bytes 262144
Async XLA Ops:
  42.9 1.6 %copy-start = (f32[8,16,256]{2,1,0:T(8,128)S(1)}, f32[8,16,256]{2,1,0:T(8,128)}, u32[]{:S(2)}) copy-start(f32[8,16,256]{2,1,0:T(8,128)} %get-tuple-element.5) | copy-start | bytes 393220

commit v3 on v2

--- a/solution.py
+++ b/solution.py
@@ -80,9 +80,16 @@
             (remote(FY.at[s, 0], HY.at[s, 1], send_h.at[s, 3], recv_h.at[s, 3], to_dn_y), inner[2], inner[3]),
         )
 
-    def start(s):
-        for copy, sends, _ in copies(s):
+    def start(s, *which):
+        given = copies(s)
+        for k in which or range(len(given)):
+            copy, sends, _ = given[k]
             pl.when(sends)(copy.start)
+
+    def put_and_start(s, x, v):
+        put(s, x, v)
+        if x in (0, X - 1):
+            start(s, 1 if x == 0 else 0)
 
     def arrive(s, along):
         for copy, _, receives in copies(s)[2 * along:2 * along + 2]:
@@ -153,13 +160,13 @@
     start(0)
 
     for x in planes(0):
-        put(1, x, apply(0, x) * (1.0 / HALF))
-    start(1)
+        put_and_start(1, x, apply(0, x) * (1.0 / HALF))
+    start(1, 2, 3)
 
     def step(s, carry):
         for x in planes(s):
-            put(s + 1, x, apply(s, x) * (2.0 / HALF) - D[s - 1, x])
-        start(s + 1)
+            put_and_start(s + 1, x, apply(s, x) * (2.0 / HALF) - D[s - 1, x])
+        start(s + 1, 2, 3)
         return carry
 
     step(1, 0)

time: 45.4 us -> 45.3 us (level)
  no operation moved by 1% of the time
where the time goes in v3:
time: 45.3 us; the launch traced here: 45.1 us
  Pallas kernels  42.2 us (93%)
  local copies, waits for them, and re-layouts  2.26 us (5%)
  between operations  0.65 us (1%)
    pallas_call x1, Pallas kernels, shards(): pl.pallas_call(functools.partial(kernel, nx, ny), out_shape=(block, block...  42.2 us
    unnamed x4, local copies, waits for them, and re-layouts  2.26 us

profile of v3, /device:TPU:0, one launch (start us, length us, event | category | flops | bytes accessed | tf_op | source)
XLA Modules:
  0.0 45.1 jit_solution(5631386153932030029)
XLA Ops:
  0.6 42.2 %shard_map.86 = (f32[8,16,256]{2,1,0:T(8,128)}, f32[8,16,256]{2,1,0:T(8,128)}) custom-call(f32[2]{0:T(128)} %low_in.1, f32[2]{0:T(128)} %high_in.1, f32[8,16,256]{2,1,0:T(8,128)} %b_in.1, f32[8,16,256]{2,1,0:T(8,128)} %sh_in.1, f32[8,16,256]{2,1,0:T(8,128)} %cx_in.1, f32[8,16,256]{2,1,0:T(8,128)} %cy_in.1, f32[8,16,256]{2,1,0:T(8,128)} %cz_in.1), custom_call_target="tpu_custom_call" | custom-call | tf_op jit(solution)/shard_map/pallas_call | solution.py:252
  42.9 0.0 copy-start
  42.9 1.6 %copy.11 = f32[8,16,256]{2,1,0:T(8,128)} copy(f32[8,16,256]{2,1,0:T(8,128)} %get-tuple-element.4) | data formatting | bytes 262144
  44.5 0.0 copy-done
  44.5 0.7 %copy.12 = f32[8,16,256]{2,1,0:T(8,128)} copy(f32[8,16,256]{2,1,0:T(8,128)S(1)} %copy-done) | data formatting | bytes 262144
Async XLA Ops:
  42.9 1.6 %copy-start = (f32[8,16,256]{2,1,0:T(8,128)S(1)}, f32[8,16,256]{2,1,0:T(8,128)}, u32[]{:S(2)}) copy-start(f32[8,16,256]{2,1,0:T(8,128)} %get-tuple-element.5) | copy-start | bytes 393220

commit v4 on v2

--- a/solution.py
+++ b/solution.py
@@ -13,7 +13,7 @@
 
 
 def kernel(nx, ny, low_in, high_in, b_in, sh_in, cx_in, cy_in, cz_in, p_ref, q_ref,
-           low_ref, high_ref, b_ref, sh_ref, cx_ref, cy_ref, cz_ref, in_sem, CO,
+           low_ref, high_ref, b_ref, sh_ref, cx_ref, cy_ref, cz_ref, in_sem, CO, FM, send_m, recv_m,
            D, HX, HY, FY, M, LXH, LYH, SY, LY, LZ, CZ, DG, G1, G2, L1, L2,
            send_h, recv_h, send_c, recv_c, send_1, recv_1, send_2, recv_2):
     X, Y, Z = b_ref.shape
@@ -23,6 +23,9 @@
         pl.semaphore_signal(barrier, inc=1, device_id=(lax.rem(ix + o, nx), iy), device_id_type=MESH)
     for o in range(1, ny):
         pl.semaphore_signal(barrier, inc=1, device_id=(ix, lax.rem(iy + o, ny)), device_id_type=MESH)
+    for o in (1, ny - 1):
+        to = (nx - 1 - ix, lax.rem(iy + o, ny))
+        pl.semaphore_signal(barrier, inc=1, device_id=to, device_id_type=MESH)
     pairs = ((cx_in, cx_ref), (cy_in, cy_ref), (b_in, b_ref), (cz_in, cz_ref), (sh_in, sh_ref),
              (low_in, low_ref), (high_in, high_ref))
     loads = [pltpu.make_async_copy(src, dst, in_sem.at[k]) for k, (src, dst) in enumerate(pairs)]
@@ -54,7 +57,12 @@
     for x in range(X):
         SY[pl.ds(x, 1), :] = cy_ref[x, Y - 1:Y, :]
     loads[2].wait()
-    pl.semaphore_wait(barrier, nx + ny - 2)
+    for x in range(X):
+        for side, y in ((0, 0), (1, Y - 1)):
+            edge = b_ref[x, y:y + 1, :]
+            FY[0, side, 0, pl.ds(x, 1), :] = edge
+            FM[side, pl.ds(X - 1 - x, 1), :] = edge
+    pl.semaphore_wait(barrier, nx + ny)
 
     def remote(src, dst, send, recv, to):
         return pltpu.make_async_remote_copy(
@@ -70,7 +78,26 @@
     coef_y = remote(SY, LYH, send_c.at[1], recv_c.at[1], to_up_y)
     pl.when(inner[1])(coef_x.start)
     pl.when(inner[3])(coef_y.start)
+    far = lax.rem(2 * nx - ix, nx), lax.rem(2 * nx - 2 - ix, nx)
+    early = (
+        (remote(b_ref.at[X - 1], HX.at[0, 0, 0], send_h.at[0, 0], recv_h.at[0, 0], to_up_x), inner[1], inner[0]),
+        (remote(b_ref.at[0], HX.at[0, 1, 0], send_h.at[0, 1], recv_h.at[0, 1], to_dn_x), inner[0], inner[1]),
+        (remote(b_ref.at[0], HX.at[0, 0, 1], send_m.at[0], recv_m.at[0], (far[0], iy)),
+         (ix > 0) & (2 * ix != nx), inner[0]),
+        (remote(b_ref.at[X - 1], HX.at[0, 1, 1], send_m.at[1], recv_m.at[1], (far[1], iy)),
+         (ix < nx - 1) & (2 * ix != nx - 2), inner[1]),
+        (remote(FY.at[0, 1, 0], HY.at[0, 0, 0], send_h.at[0, 2], recv_h.at[0, 2], to_up_y), inner[3], inner[2]),
+        (remote(FY.at[0, 0, 0], HY.at[0, 1, 0], send_h.at[0, 3], recv_h.at[0, 3], to_dn_y), inner[2], inner[3]),
+        (remote(FM.at[1], HY.at[0, 0, 1], send_m.at[2], recv_m.at[2], (nx - 1 - ix, to_up_y[1])), inner[3], inner[2]),
+        (remote(FM.at[0], HY.at[0, 1, 1], send_m.at[3], recv_m.at[3], (nx - 1 - ix, to_dn_y[1])), inner[2], inner[3]),
+    )
+    own = (pltpu.make_async_copy(b_ref.at[0], HX.at[0, 0, 1], recv_m.at[0]),
+           pltpu.make_async_copy(b_ref.at[X - 1], HX.at[0, 1, 1], recv_m.at[1]))
     mirror.start()
+    for copy, sends, _ in early:
+        pl.when(sends)(copy.start)
+    pl.when(2 * ix == nx)(own[0].start)
+    pl.when(2 * ix == nx - 2)(own[1].start)
 
     def copies(s):
         return (
@@ -149,10 +176,11 @@
 
     mirror.wait_recv()
     for x in range(X):
-        put(0, x, jnp.stack([b_ref[x], M[X - 1 - x]]))
-    start(0)
-
-    for x in planes(0):
+        D[0, x] = jnp.stack([b_ref[x], M[X - 1 - x]])
+    for copy, _, receives in early:
+        pl.when(receives)(copy.wait_recv)
+
+    for x in range(X):
         put(1, x, apply(0, x) * (1.0 / HALF))
     start(1)
 
@@ -223,7 +251,9 @@
             pl.when(sends)(copy.wait_send)
         return carry
 
-    lax.fori_loop(0, ITERS, drain, 0)
+    lax.fori_loop(1, ITERS, drain, 0)
+    for copy, sends, _ in early:
+        pl.when(sends)(copy.wait_send)
     mirror.wait_send()
     pl.when(inner[1])(coef_x.wait_send)
     pl.when(inner[3])(coef_y.wait_send)
@@ -252,6 +282,7 @@
                 cells, cells, cells, cells, cells,
                 dma((7,)),
                 pltpu.VMEM((S + 1, 2, 2, 1, Z), f32),
+                pltpu.VMEM((2, X, Z), f32), dma((4,)), dma((4,)),
                 pltpu.VMEM((S, X, 2, Y, Z), f32),
                 pltpu.VMEM((S, 2, 2, Y, Z), f32),
                 pltpu.VMEM((S, 2, 2, X, Z), f32),

time: 45.4 us -> 44.1 us (0.971)
  Pallas kernels: 42.3 us -> 41 us
    pallas_call x1, Pallas kernels: 42.3 us -> 41 us  [shards(): pl.pallas_call(functools.partial(kernel, nx, ny), out_shape=(block, block...]
where the time goes in v4:
time: 44.1 us; the launch traced here: 43.9 us
  Pallas kernels  41 us (93%)
  local copies, waits for them, and re-layouts  2.26 us (5%)
  between operations  0.65 us (1%)
    pallas_call x1, Pallas kernels, shards(): pl.pallas_call(functools.partial(kernel, nx, ny), out_shape=(block, block...  41 us
    unnamed x4, local copies, waits for them, and re-layouts  2.26 us

profile of v4, /device:TPU:0, one launch (start us, length us, event | category | flops | bytes accessed | tf_op | source)
XLA Modules:
  0.0 43.9 jit_solution(16325580843062820921)
XLA Ops:
  0.6 41.0 %shard_map.86 = (f32[8,16,256]{2,1,0:T(8,128)}, f32[8,16,256]{2,1,0:T(8,128)}) custom-call(f32[2]{0:T(128)} %low_in.1, f32[2]{0:T(128)} %high_in.1, f32[8,16,256]{2,1,0:T(8,128)} %b_in.1, f32[8,16,256]{2,1,0:T(8,128)} %sh_in.1, f32[8,16,256]{2,1,0:T(8,128)} %cx_in.1, f32[8,16,256]{2,1,0:T(8,128)} %cy_in.1, f32[8,16,256]{2,1,0:T(8,128)} %cz_in.1), custom_call_target="tpu_custom_call" | custom-call | tf_op jit(solution)/shard_map/pallas_call | solution.py:275
  41.6 0.0 copy-start
  41.6 1.6 %copy.11 = f32[8,16,256]{2,1,0:T(8,128)} copy(f32[8,16,256]{2,1,0:T(8,128)} %get-tuple-element.4) | data formatting | bytes 262144
  43.2 0.0 copy-done
  43.2 0.7 %copy.12 = f32[8,16,256]{2,1,0:T(8,128)} copy(f32[8,16,256]{2,1,0:T(8,128)S(1)} %copy-done) | data formatting | bytes 262144
Async XLA Ops:
  41.6 1.6 %copy-start = (f32[8,16,256]{2,1,0:T(8,128)S(1)}, f32[8,16,256]{2,1,0:T(8,128)}, u32[]{:S(2)}) copy-start(f32[8,16,256]{2,1,0:T(8,128)} %get-tuple-element.5) | copy-start | bytes 393220
